TPU v7x, 32 devices: a whole 2x2x4 slice. The times are simulated.
32 devices in a mesh: enc: 8 (over y, x, core), abs: 4 (over z).
Axes of the slice: x: 2, y: 2, z: 4, core: 2. Of those that a mesh axis runs over, the one named last changes fastest.
Arguments:
- tiles: bfloat16 [192, 24, 24, 1024], P('enc', None, None, 'abs'), may hold values from -6 to 6
- w_in: bfloat16 [1024, 1024], replicated, may hold values from -0.1875 to 0.1875
- w_out: bfloat16 [1024, 1024], replicated, may hold values from -0.1875 to 0.1875
- se_down: bfloat16 [1024, 256], replicated, may hold values from -0.1875 to 0.1875
- se_up: bfloat16 [256, 1024], replicated, may hold values from -0.375 to 0.375
- kernel: bfloat16 [9, 1024], replicated, may hold values from -2 to 2
- gain: bfloat16 [1024], replicated, may hold values from 0.5 to 1.5
- token_grads: bfloat16 [320, 144, 1024], P(('enc', 'abs')), may hold values from -6 to 6
- tile_counts: int32 [8, 8], replicated, may hold values from 1 to 9, as said below
- sample_owner: int32 [8, 8], replicated, may hold values from 0 to 7, as said below
- sample_rank: int32 [8, 8], replicated, may hold values from 0 to 7, as said below
Outputs:
- visual: bfloat16 [320, 144, 1024], P(('enc', 'abs'))
- tile_grads: bfloat16 [192, 24, 24, 1024], P('enc', None, None, 'abs')
- w_in_grad: float32 [1024, 1024], P(('enc', 'abs'))
- w_out_grad: float32 [1024, 1024], P(('enc', 'abs'))
- se_down_grad: float32 [1024, 256], P(('enc', 'abs'))
- se_up_grad: float32 [256, 1024], P(('enc', 'abs'))
- kernel_grad: float32 [9, 1024], P(None, ('enc', 'abs'))
- gain_grad: float32 [1024], P(('enc', 'abs'))
Inputs may be any that keep to these rules, and one draw needn't show every extreme that they name: `tile_counts`: the samples of every encoder group hold 24 tiles together; the samples owned by one abstractor group hold at most 40 tiles together. `sample_owner`: every row names each abstractor group once. `sample_rank`: the 8 samples owned by one abstractor group have distinct ranks.
All inputs are finite; a program needn't handle non-finite values.
Results may differ from a plain program's by a relative error of at most 0.0066.
Values may be sent and summed in bfloat16 or wider, within the bound.
A program may use at most 192 MiB of HBM per device.

v0:
```python
import functools
import math

import jax
import jax.numpy as jnp
from jax import lax
from jax.experimental import pallas as pl
from jax.experimental.pallas import tpu as pltpu
from jax.sharding import PartitionSpec as P

MOST = 9


NORM_EPS = 1e-06


def route_tables(counts, owners, ranks):
    groups = counts.shape[0]
    start = jnp.cumsum(counts, axis=1, dtype=jnp.int32) - counts
    flat_counts = counts.reshape(-1)
    flat_owners = owners.reshape(-1)
    flat_ranks = ranks.reshape(-1)
    ahead = (flat_owners[:, None] == flat_owners[None, :]) & (
        flat_ranks[None, :] < flat_ranks[:, None]
    )
    offset = jnp.sum(jnp.where(ahead, flat_counts[None, :], 0), axis=1, dtype=jnp.int32).reshape(
        groups, groups
    )
    owner_axis = jnp.arange(groups, dtype=jnp.int32)
    filled = jnp.sum(
        jnp.where(flat_owners[None, :] == owner_axis[:, None], flat_counts[None, :], 0),
        axis=1,
        dtype=jnp.int32,
    )
    return (start, offset, filled)


VMEM_BYTES = 50 * 1024 * 1024
LANES = 128


def params():
    return pltpu.CompilerParams(vmem_limit_bytes=VMEM_BYTES)


def pool_kernel(rows_ref, tile_ref, out_ref, half_ref):
    grid, channels = tile_ref.shape[1], tile_ref.shape[3]
    side = grid // 2
    wide = tile_ref[0].astype(jnp.float32).reshape(side, 2, grid, channels)
    half = (wide[:, 0] + wide[:, 1]).reshape(side * grid, channels)
    cells = side * side
    for part in range(channels // LANES):
        lanes = slice(part * LANES, (part + 1) * LANES)
        half_ref[part] = half[:, lanes]
        even = half_ref[part, pl.ds(0, cells, stride=2), :]
        odd = half_ref[part, pl.ds(1, cells, stride=2), :]
        out_ref[0, :, lanes] = ((even + odd) * 0.25).astype(jnp.bfloat16)


def pool_and_place(tiles, rows, sends):
    count, grid, _, channels = tiles.shape
    cells = (grid // 2) ** 2
    return pl.pallas_call(
        pool_kernel,
        out_shape=jax.ShapeDtypeStruct((sends, cells, channels), jnp.bfloat16),
        grid_spec=pltpu.PrefetchScalarGridSpec(
            num_scalar_prefetch=1,
            grid=(count,),
            in_specs=[pl.BlockSpec((1, grid, grid, channels), lambda g, rows: (g, 0, 0, 0))],
            out_specs=pl.BlockSpec((1, cells, channels), lambda g, rows: (rows[g], 0, 0)),
            scratch_shapes=[pltpu.VMEM((channels // LANES, 2 * cells, LANES), jnp.float32)],
        ),
        compiler_params=params(),
        name="pool_and_place",
    )(rows, tiles)


def spread_kernel(rows_ref, grads_ref, out_ref, half_ref):
    grid, channels = out_ref.shape[1], out_ref.shape[3]
    side = grid // 2
    cells = side * side
    for part in range(channels // LANES):
        lanes = slice(part * LANES, (part + 1) * LANES)
        quarter = grads_ref[0, :, lanes].astype(jnp.float32) * 0.25
        half_ref[part, pl.ds(0, cells, stride=2), :] = quarter
        half_ref[part, pl.ds(1, cells, stride=2), :] = quarter
        half = half_ref[part].reshape(side, 1, grid, LANES)
        whole = jnp.broadcast_to(half, (side, 2, grid, LANES)).reshape(grid, grid, LANES)
        out_ref[0, :, :, lanes] = whole.astype(jnp.bfloat16)


def pick_and_spread(grads, rows, grid):
    _, cells, channels = grads.shape
    count = rows.shape[0]
    return pl.pallas_call(
        spread_kernel,
        out_shape=jax.ShapeDtypeStruct((count, grid, grid, channels), jnp.bfloat16),
        grid_spec=pltpu.PrefetchScalarGridSpec(
            num_scalar_prefetch=1,
            grid=(count,),
            in_specs=[pl.BlockSpec((1, cells, channels), lambda g, rows: (rows[g], 0, 0))],
            out_specs=pl.BlockSpec((1, grid, grid, channels), lambda g, rows: (g, 0, 0, 0)),
            scratch_shapes=[pltpu.VMEM((channels // LANES, 2 * cells, LANES), jnp.float32)],
        ),
        compiler_params=params(),
        name="pick_and_spread",
    )(rows, grads)


def copy_kernel(rows_ref, source_ref, out_ref, sems):
    count = out_ref.shape[0]

    def one(g):
        return pltpu.make_async_copy(source_ref.at[rows_ref[g]], out_ref.at[g], sems.at[g])

    @pl.loop(0, count)
    def _(g):
        one(g).start()

    @pl.loop(0, count)
    def _(g):
        one(g).wait()


def pick_rows(source, rows):
    count = rows.shape[0]
    return pl.pallas_call(
        copy_kernel,
        out_shape=jax.ShapeDtypeStruct((count,) + source.shape[1:], source.dtype),
        grid_spec=pltpu.PrefetchScalarGridSpec(
            num_scalar_prefetch=1,
            grid=(),
            in_specs=[pl.BlockSpec(memory_space=pl.ANY)],
            out_specs=pl.BlockSpec(memory_space=pltpu.VMEM),
            scratch_shapes=[pltpu.SemaphoreType.DMA((count,))],
        ),
        compiler_params=params(),
        name="pick_rows",
    )(rows, source)


def place_kernel(rows_ref, live_ref, source_ref, out_ref, sems):
    count = source_ref.shape[0]

    def one(g):
        return pltpu.make_async_copy(source_ref.at[g], out_ref.at[rows_ref[g]], sems.at[g])

    @pl.loop(0, count)
    def _(g):
        @pl.when(live_ref[g] > 0)
        def _():
            one(g).start()

    @pl.loop(0, count)
    def _(g):
        @pl.when(live_ref[g] > 0)
        def _():
            one(g).wait()


def place_rows(source, rows, live, sends):
    count = rows.shape[0]
    return pl.pallas_call(
        place_kernel,
        out_shape=jax.ShapeDtypeStruct((sends,) + source.shape[1:], source.dtype),
        grid_spec=pltpu.PrefetchScalarGridSpec(
            num_scalar_prefetch=2,
            grid=(),
            in_specs=[pl.BlockSpec(memory_space=pltpu.VMEM)],
            out_specs=pl.BlockSpec(memory_space=pl.ANY),
            scratch_shapes=[pltpu.SemaphoreType.DMA((count,))],
        ),
        compiler_params=params(),
        name="place_rows",
    )(rows, live, source)


def exchange_kernel(axes, sizes, *refs):
    jobs = len(axes)
    sources, targets = refs[:jobs], refs[jobs : 2 * jobs]
    held, sems = refs[2 * jobs : 3 * jobs], refs[3 * jobs :]
    barrier = pltpu.get_barrier_semaphore()
    names = sorted(set(axes))
    peers = 0
    for axis in names:
        me, size = lax.axis_index(axis), sizes[axis]
        for step in range(1, size):
            pl.semaphore_signal(
                barrier,
                inc=1,
                device_id={axis: lax.rem(me + step, size)},
                device_id_type=pl.DeviceIdType.MESH,
            )
        peers += size - 1
    pl.semaphore_wait(barrier, peers)
    remote, own = [], []
    for job, axis in enumerate(axes):
        me, size = lax.axis_index(axis), sizes[axis]
        send, recv, local_sem = sems[3 * job : 3 * job + 3]
        for step in range(1, size):
            peer = lax.rem(me + step, size)
            copy = pltpu.make_async_remote_copy(
                src_ref=sources[job].at[peer],
                dst_ref=targets[job].at[me],
                send_sem=send.at[step],
                recv_sem=recv.at[step],
                device_id={axis: peer},
                device_id_type=pl.DeviceIdType.MESH,
            )
            copy.start()
            arriving = pltpu.make_async_remote_copy(
                src_ref=sources[job].at[peer],
                dst_ref=targets[job].at[lax.rem(me + size - step, size)],
                send_sem=send.at[step],
                recv_sem=recv.at[step],
                device_id={axis: peer},
                device_id_type=pl.DeviceIdType.MESH,
            )
            remote.append((copy, arriving))
        take = pltpu.make_async_copy(sources[job].at[me], held[job], local_sem)
        keep = pltpu.make_async_copy(held[job], targets[job].at[me], local_sem)
        take.start()
        own.append((take, keep))
    for take, keep in own:
        take.wait()
        keep.start()
    for take, keep in own:
        keep.wait()
    for copy, arriving in remote:
        copy.wait_send()
        arriving.wait_recv()


def exchange(arrays, axes, sizes, collective_id):
    scratch = [pltpu.VMEM(a.shape[1:], a.dtype) for a in arrays]
    for axis in axes:
        scratch += [pltpu.SemaphoreType.DMA((sizes[axis],))] * 2 + [pltpu.SemaphoreType.DMA]
    return pl.pallas_call(
        functools.partial(exchange_kernel, axes, sizes),
        out_shape=tuple(jax.ShapeDtypeStruct(a.shape, a.dtype) for a in arrays),
        in_specs=[pl.BlockSpec(memory_space=pl.ANY)] * len(arrays),
        out_specs=tuple(pl.BlockSpec(memory_space=pl.ANY) for _ in arrays),
        scratch_shapes=scratch,
        compiler_params=pltpu.CompilerParams(
            collective_id=collective_id, has_side_effects=True
        ),
        name="exchange",
    )(*arrays)


def edge_masks(cells, side):
    row = lax.broadcasted_iota(jnp.int32, (cells, LANES), 0)
    col = lax.rem(row, side)
    one = lambda keep: keep.astype(jnp.float32)
    return (
        one(row >= side),
        one(row < cells - side),
        one(col >= 1),
        one(col < side - 1),
    )


def row_neighbours(field, masks, side):
    cells = field.shape[0]
    above = pltpu.roll(field, side, 0) * masks[0]
    below = pltpu.roll(field, cells - side, 0) * masks[1]
    return (above, below)


def col_previous(field, masks):
    return pltpu.roll(field, 1, 0) * masks[2]


def col_next(field, masks):
    return pltpu.roll(field, field.shape[0] - 1, 0) * masks[3]


ROWS = 48


def forward_kernel(
    live_ref, owned_ref, back_ref, w_in_ref, kernel_ref, gain_ref,
    pooled_ref, normed_ref, hidden_ref, spatial_ref, squeeze_ref, excite_ref,
):
    columns, batch, cells, narrow = owned_ref.shape
    width = columns * narrow
    side = math.isqrt(cells)
    first = pl.program_id(0) * batch
    gain = gain_ref[...].astype(jnp.float32)
    for b in range(batch):
        keep = live_ref[first + b] > 0
        for r in range(0, cells, ROWS):
            rows = slice(r, r + ROWS)
            pieces = [owned_ref[c, b, rows, :] for c in range(columns)]
            pooled = jnp.concatenate(pieces, axis=-1)
            wide = jnp.where(keep, pooled.astype(jnp.float32), 0.0)
            pooled_ref[b, rows, :] = wide.astype(jnp.bfloat16)
            average = jnp.mean(wide, axis=-1, keepdims=True)
            centred = wide - average
            variance = jnp.mean(centred * centred, axis=-1, keepdims=True)
            standard = centred * lax.rsqrt(variance + NORM_EPS)
            normed_ref[b, rows, :] = (standard * gain).astype(jnp.bfloat16)
    hidden = jnp.dot(
        normed_ref[...].reshape(batch * cells, width),
        w_in_ref[...],
        preferred_element_type=jnp.float32,
    )
    hidden_ref[...] = hidden.reshape(batch, cells, width)
    masks = edge_masks(cells, side)
    for b in range(batch):

        @pl.loop(0, width // LANES)
        def _(part):
            lanes = pl.ds(pl.multiple_of(part * LANES, LANES), LANES)
            value = hidden_ref[b, :, lanes]
            act = value * jax.nn.sigmoid(value)
            above, below = row_neighbours(act, masks, side)
            taps = kernel_ref[:, lanes]
            spread = [
                taps[c : c + 1] * above + taps[3 + c : 4 + c] * act + taps[6 + c : 7 + c] * below
                for c in range(3)
            ]
            spatial = spread[1] + col_previous(spread[0], masks) + col_next(spread[2], masks)
            spatial_ref[b, :, lanes] = spatial
            mixed = spatial * jax.nn.sigmoid(spatial)
            squeeze_ref[b, :, lanes] = jnp.sum(mixed, axis=0, keepdims=True) * (1.0 / cells)
            excite_ref[b, :, lanes] = jnp.sum(
                back_ref[b, :, lanes] * mixed, axis=0, keepdims=True
            )


def forward_call(owned, back_scaled, live, w_in, taps, gain):
    columns, count, cells, narrow = owned.shape
    width = columns * narrow
    batch = 2 if count % 2 == 0 else 1
    block = lambda: pl.BlockSpec((batch, cells, width), lambda g, live: (g, 0, 0))
    row = lambda: pl.BlockSpec((batch, 1, width), lambda g, live: (g, 0, 0))
    whole = lambda a: pl.BlockSpec(a.shape, lambda g, live: (0,) * a.ndim)
    wide = lambda kind: jax.ShapeDtypeStruct((count, cells, width), kind)
    line = jax.ShapeDtypeStruct((count, 1, width), jnp.float32)
    return pl.pallas_call(
        forward_kernel,
        out_shape=(
            wide(jnp.bfloat16), wide(jnp.bfloat16), wide(jnp.float32), wide(jnp.float32), line, line,
        ),
        grid_spec=pltpu.PrefetchScalarGridSpec(
            num_scalar_prefetch=1,
            grid=(count // batch,),
            in_specs=[
                pl.BlockSpec((columns, batch, cells, narrow), lambda g, live: (0, g, 0, 0)),
                block(), whole(w_in), whole(taps), whole(gain),
            ],
            out_specs=[block(), block(), block(), block(), row(), row()],
        ),
        compiler_params=params(),
        cost_estimate=pl.CostEstimate(
            flops=2 * count * cells * width * width,
            bytes_accessed=30 * count * cells * width,
            transcendentals=4 * count * cells * width,
        ),
        name="forward",
    )(live, owned, back_scaled, w_in, taps, gain)


def backward_kernel(
    pooled_ref, hidden_ref, spatial_ref, back_ref, up_ref, excite_ref, shift_ref,
    w_in_t_ref, kernel_ref, gain_ref,
    back_hidden_ref, back_in_ref, taps_ref, gain_grad_ref, normed_ref,
):
    columns, batch, cells, narrow = back_in_ref.shape
    width = columns * narrow
    side = math.isqrt(cells)

    @pl.when(pl.program_id(0) == 0)
    def _():
        taps_ref[...] = jnp.zeros_like(taps_ref)
        gain_grad_ref[...] = jnp.zeros_like(gain_grad_ref)

    masks = edge_masks(cells, side)
    for b in range(batch):

        @pl.loop(0, width // LANES)
        def _(part):
            lanes = pl.ds(pl.multiple_of(part * LANES, LANES), LANES)
            taps = kernel_ref[:, lanes]
            spatial = spatial_ref[b, :, lanes]
            sig = jax.nn.sigmoid(spatial)
            back_mixed = back_ref[b, :, lanes] * excite_ref[b, :, lanes] + shift_ref[b, :, lanes]
            back = back_mixed * (sig * (1.0 + spatial * (1.0 - sig)))
            above, below = row_neighbours(back, masks, side)
            spread = [
                taps[c : c + 1] * below + taps[3 + c : 4 + c] * back + taps[6 + c : 7 + c] * above
                for c in range(3)
            ]
            back_act = spread[1] + col_next(spread[0], masks) + col_previous(spread[2], masks)
            value = hidden_ref[b, :, lanes]
            sig = jax.nn.sigmoid(value)
            back_hidden_ref[b, :, lanes] = (
                back_act * (sig * (1.0 + value * (1.0 - sig)))
            ).astype(jnp.bfloat16)
            act = value * sig
            above, below = row_neighbours(act, masks, side)
            sides = (
                pltpu.roll(back * masks[2], cells - 1, 0),
                back,
                pltpu.roll(back * masks[3], 1, 0),
            )
            for a, field in enumerate((above, act, below)):
                for c in range(3):
                    tap = 3 * a + c
                    taps_ref[tap : tap + 1, lanes] += jnp.sum(
                        sides[c] * field, axis=0, keepdims=True
                    )

    normed_ref[...] = jnp.dot(
        back_hidden_ref[...].reshape(batch * cells, width),
        w_in_t_ref[...],
        preferred_element_type=jnp.float32,
    )
    gain = gain_ref[...].astype(jnp.float32)
    for b in range(batch):
        for r in range(0, cells, ROWS):
            rows = slice(r, r + ROWS)
            wide = pooled_ref[b, rows, :].astype(jnp.float32)
            average = jnp.mean(wide, axis=-1, keepdims=True)
            centred = wide - average
            variance = jnp.mean(centred * centred, axis=-1, keepdims=True)
            inverse = lax.rsqrt(variance + NORM_EPS)
            standard = centred * inverse
            back_normed = normed_ref[b * cells + r : b * cells + r + ROWS, :]
            gain_grad_ref[...] += jnp.sum(back_normed * standard, axis=0, keepdims=True)
            back_x = back_normed * gain
            centre = jnp.mean(back_x, axis=-1, keepdims=True)
            along = jnp.mean(back_x * standard, axis=-1, keepdims=True)
            result = up_ref[b, rows, :].astype(jnp.float32) + inverse * (
                back_x - centre - standard * along
            )
            result = result.astype(jnp.bfloat16)
            for c in range(columns):
                back_in_ref[c, b, rows, :] = result[:, c * narrow : (c + 1) * narrow]


def backward_call(
    pooled, hidden, spatial, back_scaled, upstream, excite, shift, w_in_t, taps, gain, columns
):
    count, cells, width = pooled.shape
    narrow = width // columns
    batch = 2 if count % 2 == 0 else 1
    block = lambda: pl.BlockSpec((batch, cells, width), lambda g: (g, 0, 0))
    row = lambda: pl.BlockSpec((batch, 1, width), lambda g: (g, 0, 0))
    whole = lambda shape: pl.BlockSpec(shape, lambda g: (0,) * len(shape))
    return pl.pallas_call(
        backward_kernel,
        out_shape=(
            jax.ShapeDtypeStruct((count, cells, width), jnp.bfloat16),
            jax.ShapeDtypeStruct((columns, count, cells, narrow), jnp.bfloat16),
            jax.ShapeDtypeStruct((9, width), jnp.float32),
            jax.ShapeDtypeStruct((1, width), jnp.float32),
        ),
        grid=(count // batch,),
        in_specs=[
            block(), block(), block(), block(), block(), row(), row(),
            whole(w_in_t.shape), whole(taps.shape), whole(gain.shape),
        ],
        out_specs=[
            block(),
            pl.BlockSpec((columns, batch, cells, narrow), lambda g: (0, g, 0, 0)),
            whole((9, width)),
            whole((1, width)),
        ],
        scratch_shapes=[pltpu.VMEM((batch * cells, width), jnp.float32)],
        compiler_params=params(),
        cost_estimate=pl.CostEstimate(
            flops=2 * count * cells * width * width,
            bytes_accessed=30 * count * cells * width,
            transcendentals=4 * count * cells * width,
        ),
        name="backward",
    )(pooled, hidden, spatial, back_scaled, upstream, excite, shift, w_in_t, taps, gain)


def silu_slope(value):
    sig = jax.nn.sigmoid(value)
    return sig * (1.0 + value * (1.0 - sig))


def pick_row(table, chosen):
    return jnp.sum(jnp.where(chosen[:, None], table, 0), axis=0, dtype=jnp.int32)


def local(
    tiles,
    w_in,
    w_out,
    se_down,
    se_up,
    kernel,
    gain,
    token_grads,
    tile_counts,
    sample_owner,
    sample_rank,
):
    groups = lax.axis_size("enc")
    columns = lax.axis_size("abs")
    group_id = lax.axis_index("enc")
    column_id = lax.axis_index("abs")
    local_tiles = tiles.shape[0]
    owned_rows = token_grads.shape[0]
    capacity = owned_rows * columns
    cells = token_grads.shape[1]
    start, offset, filled = route_tables(tile_counts, sample_owner, sample_rank)
    sources = jnp.arange(groups, dtype=jnp.int32)
    this_group = sources == group_id
    owner_row = pick_row(sample_owner, this_group)
    start_row = pick_row(start, this_group)
    arriving = sample_owner == group_id
    recv_count = jnp.sum(jnp.where(arriving, tile_counts, 0), axis=1, dtype=jnp.int32)
    recv_offset = jnp.sum(jnp.where(arriving, offset, 0), axis=1, dtype=jnp.int32)
    positions = jnp.arange(capacity, dtype=jnp.int32)
    inside = (positions[:, None] >= recv_offset[None, :]) & (
        positions[:, None] < (recv_offset + recv_count)[None, :]
    )
    gather_rows = jnp.sum(
        jnp.where(inside, sources[None, :] * MOST + positions[:, None] - recv_offset[None, :], 0),
        axis=1,
        dtype=jnp.int32,
    )
    occupied = jnp.any(inside, axis=1).astype(jnp.int32)
    tile_ids = jnp.arange(local_tiles, dtype=jnp.int32)
    member = (
        jnp.sum(
            (start_row[None, :] <= tile_ids[:, None]).astype(jnp.int32), axis=1, dtype=jnp.int32
        )
        - 1
    )
    which = member[:, None] == sources[None, :]
    member_owner = jnp.sum(jnp.where(which, owner_row[None, :], 0), axis=1, dtype=jnp.int32)
    member_start = jnp.sum(jnp.where(which, start_row[None, :], 0), axis=1, dtype=jnp.int32)
    unpack_rows = member_owner * MOST + tile_ids - member_start
    filled_here = jnp.sum(jnp.where(this_group, filled, 0), dtype=jnp.int32)
    live = column_id * owned_rows + jnp.arange(owned_rows, dtype=jnp.int32) < filled_here
    width = token_grads.shape[2]
    narrow = tiles.shape[3]
    devices = groups * columns
    flat = (owned_rows * cells, width)
    upstream = jnp.where(live[:, None, None], token_grads, jnp.zeros_like(token_grads))
    back_scaled = jnp.dot(
        upstream.reshape(flat), w_out.T, preferred_element_type=jnp.float32
    ).reshape(upstream.shape)
    taps = kernel.astype(jnp.float32)
    gain_row = gain.reshape(1, width)

    sends = groups * MOST
    send = pool_and_place(tiles, unpack_rows, sends).reshape(groups, MOST, cells, narrow)
    received = lax.all_to_all(send, "enc", split_axis=0, concat_axis=0, tiled=True)
    compact = pick_rows(received.reshape(groups * MOST, cells, narrow), gather_rows)
    owned = lax.all_to_all(
        compact.reshape(columns, owned_rows, cells, narrow),
        "abs",
        split_axis=0,
        concat_axis=0,
        tiled=True,
    )
    pooled, normed, hidden, spatial, squeeze, back_excite = forward_call(
        owned, back_scaled, live.astype(jnp.int32), w_in, taps, gain_row
    )

    exact = functools.partial(jnp.dot, precision=lax.Precision.HIGHEST)
    squeeze = squeeze.reshape(owned_rows, width)
    down, up = se_down.astype(jnp.float32), se_up.astype(jnp.float32)
    squeeze_pre = exact(squeeze, down)
    squeeze_act = jax.nn.silu(squeeze_pre)
    excite = jax.nn.sigmoid(exact(squeeze_act, up))
    back_pre = back_excite.reshape(owned_rows, width) * excite * (1.0 - excite)
    back_squeeze_pre = exact(back_pre, up.T) * silu_slope(squeeze_pre)
    shift = exact(back_squeeze_pre, down.T) / cells

    back_hidden, back_in, taps_term, gain_term = backward_call(
        pooled, hidden, spatial, back_scaled, upstream,
        excite[:, None, :], shift[:, None, :], w_in.T, taps, gain_row, columns,
    )
    scaled = (jax.nn.silu(spatial) * excite[:, None, :]).astype(jnp.bfloat16)
    output = jnp.dot(scaled.reshape(flat), w_out, preferred_element_type=jnp.float32)
    visual = (pooled.astype(jnp.float32) + output.reshape(pooled.shape)).astype(jnp.bfloat16)

    w_out_term = jnp.dot(
        scaled.reshape(flat).T, upstream.reshape(flat), preferred_element_type=jnp.float32
    )
    w_in_term = jnp.dot(
        normed.reshape(flat).T, back_hidden.reshape(flat), preferred_element_type=jnp.float32
    )
    se_up_term = exact(squeeze_act.T, back_pre)
    se_down_term = exact(squeeze.T, back_squeeze_pre)
    share = width // devices
    small = jnp.concatenate(
        [
            taps_term.reshape(9, devices, share).transpose(1, 0, 2).reshape(devices, 9 * share),
            gain_term.reshape(devices, share),
        ],
        axis=1,
    )
    lines = -(-10 * share // width)
    small = jnp.pad(small, ((0, 0), (0, lines * width - 10 * share)))
    dest = lambda term: term.astype(jnp.bfloat16).reshape(groups, columns, -1, width)
    rest = jnp.concatenate([dest(se_down_term), dest(se_up_term), dest(small)], axis=2)

    sizes = {"enc": groups, "abs": columns}
    back_narrow, *partial = exchange(
        [
            back_in,
            w_in_term.astype(jnp.bfloat16).reshape(groups, -1, width),
            w_out_term.astype(jnp.bfloat16).reshape(groups, -1, width),
            rest,
        ],
        ("abs", "enc", "enc", "enc"),
        sizes,
        1,
    )
    returned = place_rows(
        back_narrow.reshape(capacity, cells, narrow), gather_rows, occupied, sends
    )
    partial = [
        jnp.sum(part.astype(jnp.float32), axis=0)
        .astype(jnp.bfloat16)
        .reshape(columns, -1, width)
        for part in partial
    ]
    arrived, *parts = exchange(
        [returned.reshape(groups, MOST, cells, narrow)] + partial,
        ("enc", "abs", "abs", "abs"),
        sizes,
        2,
    )
    tile_grads = pick_and_spread(
        arrived.reshape(sends, cells, narrow), unpack_rows, tiles.shape[1]
    )
    w_in_sum, w_out_sum, rest_sum = [
        jnp.sum(part.astype(jnp.float32), axis=0) for part in parts
    ]
    down_rows = se_down.size // (devices * width)
    up_rows = se_up.size // (devices * width)
    scale = 1.0 / math.sqrt(groups * local_tiles * cells)
    lasts = rest_sum[down_rows + up_rows :].reshape(-1)
    return (
        visual,
        tile_grads,
        w_in_sum * scale,
        w_out_sum * scale,
        rest_sum[:down_rows].reshape(-1, se_down.shape[1]) * scale,
        rest_sum[down_rows : down_rows + up_rows] * scale,
        lasts[: 9 * share].reshape(9, share) * scale,
        lasts[9 * share : 10 * share] * scale,
    )


def solution(mesh):
    return jax.shard_map(
        local,
        mesh=mesh,
        in_specs=(
            P("enc", None, None, "abs"),
            P(),
            P(),
            P(),
            P(),
            P(),
            P(),
            P(("enc", "abs"), None, None),
            P(),
            P(),
            P(),
        ),
        out_specs=(
            P(("enc", "abs"), None, None),
            P("enc", None, None, "abs"),
            P(("enc", "abs"), None),
            P(("enc", "abs"), None),
            P(("enc", "abs"), None),
            P(("enc", "abs"), None),
            P(None, ("enc", "abs")),
            P(("enc", "abs")),
        ),
        check_vma=False,
    )
```

profile of v0, /device:TPU:0, one launch (start us, length us, event | category | flops | bytes accessed | tf_op | source)
XLA Modules:
  0.0 394.5 jit_solution(11717086982533900896)
XLA Ops:
  0.7 0.9 eq.59
  1.6 0.8 broadcast_in_dim.104
  2.3 0.8 lt.38
  3.4 0.9 reduce_window_sum.11
  4.2 0.9 select_reduce_fusion.4
  5.3 15.1 %pool_and_place.1 = bf16[72,144,256]{2,1,0:T(8,128)(2,1)} custom-call(s32[24]{0:T(128)S(1)} %add_subtract_fusion.rows_ref, bf16[24,24,24,256]{3,2,1,0:T(8,128)(2,1)} %tile_ref.1), custom_call_target="tpu_custom_call" | custom-call | tf_op jit(solution)/shard_map/pool_and_place/pallas_call | solution.py:63
  20.4 5.2 %all-to-all-start = ((bf16[8,9,144,256]{3,2,1,0:T(8,128)(2,1)}), bf16[8,9,144,256]{3,2,1,0:T(8,128)(2,1)}, u32[]{:S(2)}, u32[]{:S(2)}) async-start(bf16[8,9,144,256]{3,2,1,0:T(8,128)(2,1)} %bitcast.51), calls=%async_computation | async-start | bytes 10616832 | tf_op jit(solution)/shard_map/all_to_all | solution.py:556
  25.7 61.1 %all-to-all-done = bf16[8,9,144,256]{3,2,1,0:T(8,128)(2,1)} async-done(((bf16[8,9,144,256]{3,2,1,0:T(8,128)(2,1)}), bf16[8,9,144,256]{3,2,1,0:T(8,128)(2,1)}, u32[]{:S(2)}, u32[]{:S(2)}) %all-to-all-start) | async-done | bytes 5308448 | tf_op jit(solution)/shard_map/all_to_all | solution.py:556
  86.8 2.8 pick_rows.1
  89.6 1.6 copy-done.2
  91.2 5.8 %all-to-all-start.1 = ((bf16[4,10,144,256]{3,2,1,0:T(8,128)(2,1)}), bf16[4,10,144,256]{3,2,1,0:T(8,128)(2,1)}, u32[]{:S(2)}, u32[]{:S(2)}) async-start(bf16[4,10,144,256]{3,2,1,0:T(8,128)(2,1)} %bitcast.47), calls=%async_computation.1 | async-start | bytes 5898240 | tf_op jit(solution)/shard_map/all_to_all | solution.py:558
  97.1 4.0 %copy.30 = bf16[1024,1024]{0,1:T(8,128)(2,1)} copy(bf16[1024,1024]{1,0:T(8,128)(2,1)} %w_in_ref.1) | data formatting | bytes 4194304 | tf_op args[1]
  101.2 0.6 select_reduce_fusion.9
  101.9 0.7 fusion.27
  102.5 2.1 broadcast_select_fusion.up_ref
  104.6 1.6 copy-done.6
  106.3 5.2 %fusion.1.back_ref = f32[10,144,1024]{2,1,0:T(8,128)} fusion(bf16[10,144,1024]{2,1,0:T(8,128)(2,1)S(1)} %broadcast_select_fusion.up_ref, bf16[1024,1024]{1,0:T(8,128)(2,1)S(1)} %copy-done), kind=kOutput, calls=%fused_computation.6 | convolution fusion | flops 3019898880 | bytes 10944512 | tf_op jit(solution)/shard_map/dot_general | solution.py:548
  111.5 49.1 %all-to-all-done.1.owned_ref = bf16[4,10,144,256]{3,2,1,0:T(8,128)(2,1)} async-done(((bf16[4,10,144,256]{3,2,1,0:T(8,128)(2,1)}), bf16[4,10,144,256]{3,2,1,0:T(8,128)(2,1)}, u32[]{:S(2)}, u32[]{:S(2)}) %all-to-all-start.1) | async-done | bytes 2949152 | tf_op jit(solution)/shard_map/all_to_all | solution.py:558
  160.6 1.6 copy-done.5
  162.2 17.9 %forward.1 = (bf16[10,144,1024]{2,1,0:T(8,128)(2,1)}, bf16[10,144,1024]{2,1,0:T(8,128)(2,1)}, f32[10,144,1024]{2,1,0:T(8,128)}, f32[10,144,1024]{2,1,0:T(8,128)}...) custom-call(s32[10]{0:T(128)S(1)} %get-tuple-element.50.live_ref, ...), custom_call_target="tpu_custom_call" | custom-call | flops 3019898880 | bytes 44236800 | tf_op jit(solution)/shard_map/forward/pallas_call | solution.py:341
  180.1 0.3 fusion.11
  180.5 0.3 fusion.5
  180.9 0.5 convolution_multiply_fusion.1
  181.4 1.1 convolution_convert_fusion
  182.4 0.5 convolution_multiply_fusion
  183.0 1.0 convolution_convert_fusion.1
  184.1 7.7 %bitcast_convert_fusion = bf16[1024,1024]{1,0:T(8,128)(2,1)} fusion(bf16[10,144,1024]{2,1,0:T(8,128)(2,1)S(1)} %copy-done.7, f32[10,144,1024]{2,1,0:T(8,128)} %get-tuple-element.27.spatial_ref, f32[10,1024]{1,0:T(8,128)S(1)} %fusion.5), kind=kOutput, calls=%fused_computation.2 | convolution fusion | flops 3029794816 | bytes 10985472 | tf_op jit(solution)/shard_map/dot_general | solution.py:587
  191.8 4.8 %add_convert_fusion = bf16[10,144,1024]{2,1,0:T(8,128)(2,1)} fusion(bf16[10,144,1024]{2,1,0:T(8,128)(2,1)S(1)} %copy-done.8, bf16[1024,1024]{1,0:T(8,128)(2,1)S(1)} %copy-done, f32[10,144,1024]{2,1,0:T(8,128)S(1)} %bitcast.53, f32[10,1024]{1,0:T(8,128)S(1)} %fusion.5), kind=kOutput, calls=%fused_computation | convolution fusion | flops 3033169920 | bytes 13934592 | tf_op jit(solution)/shard_map/dot_general | solution.py:584
  196.6 26.4 %backward.1 = (bf16[10,144,1024]{2,1,0:T(8,128)(2,1)}, bf16[4,10,144,256]{3,2,1,0:T(8,128)(2,1)}, f32[9,1024]{1,0:T(8,128)S(1)}, f32[1,1024]{1,0:T(1,128)S(1)}) custom-call(bf16[10,144,1024]{2,1,0:T(8,128)(2,1)} %get-tuple-element.26.pooled_ref, f32[10,144,1024]{2,1,0:T(8,128)} %get-tuple-element.29.hidden_ref, ...), custom_call_target="tpu_custom_call" | custom-call | flops 3019898880 | bytes 44236800 | tf_op jit(solution)/shard_map/backward/pallas_call | solution.py:452
  223.7 0.3 reshape.143
  224.0 7.5 %bitcast_convert_fusion.1 = bf16[1024,1024]{1,0:T(8,128)(2,1)} fusion(bf16[10,144,1024]{2,1,0:T(8,128)(2,1)} %get-tuple-element.32, bf16[10,144,1024]{2,1,0:T(8,128)(2,1)} %get-tuple-element.33), kind=kOutput, calls=%fused_computation.3 | convolution fusion | flops 3020947456 | bytes 7995392 | tf_op jit(solution)/shard_map/dot_general | solution.py:590
  231.5 1.5 pad_maximum_fusion.refs_3_
  233.0 68.1 %exchange.2 = (bf16[4,10,144,256]{3,2,1,0:T(8,128)(2,1)}, bf16[8,128,1024]{2,1,0:T(8,128)(2,1)}, bf16[8,128,1024]{2,1,0:T(8,128)(2,1)}, bf16[8,4,17,1024]{3,2,1,0:T(8,128)(2,1)}) custom-call(bf16[4,10,144,256]{3,2,1,0:T(8,128)(2,1)} %get-tuple-element.31.refs_0_, bf16[8,128,1024]{2,1,0:T(8,128)(2,1)} %bitcast.57, bf16[8,128,1024]{2,1,0:T(8,128)(2,1)} %bitcast.56, ...), custom_call_target="tpu_custom_call" | custom-call | tf_op jit(solution)/shard_map/exchange/pallas_call | solution.py:238
  301.1 2.6 reduce_sum.175.refs_3_
  303.6 2.7 reduce_sum.173
  306.4 1.1 reduce_sum.174
  307.5 1.8 copy-done.4
  309.3 2.5 place_rows.1
  311.8 61.6 %exchange.3 = (bf16[8,9,144,256]{3,2,1,0:T(8,128)(2,1)}, bf16[4,32,1024]{2,1,0:T(8,128)(2,1)}, bf16[4,32,1024]{2,1,0:T(8,128)(2,1)}, bf16[4,17,1024]{2,1,0:T(8,128)(2,1)}) custom-call(bf16[8,9,144,256]{3,2,1,0:T(8,128)(2,1)} %bitcast.50, bf16[4,32,1024]{2,1,0:T(8,128)(2,1)} %bitcast.58, bf16[4,32,1024]{2,1,0:T(8,128)(2,1)} %bitcast.59, ...), custom_call_target="tpu_custom_call" | custom-call | tf_op jit(solution)/shard_map/exchange/pallas_call | solution.py:238
  373.4 1.0 convert_reduce_fusion.2
  374.3 0.6 fusion.23
  374.9 0.6 slice_multiply_fusion
  375.6 0.7 mul.102
  376.2 0.6 mul.98
  376.9 1.1 convert_reduce_fusion
  378.0 0.7 broadcast_multiply_fusion
  378.7 0.7 broadcast_multiply_fusion.1
  379.3 15.1 %pick_and_spread.1 = bf16[24,24,24,256]{3,2,1,0:T(8,128)(2,1)} custom-call(s32[24]{0:T(128)S(1)} %add_subtract_fusion.rows_ref, bf16[72,144,256]{2,1,0:T(8,128)(2,1)} %bitcast.54), custom_call_target="tpu_custom_call" | custom-call | tf_op jit(solution)/shard_map/pick_and_spread/pallas_call | solution.py:95
  (55 shorter events, 1.5 us)
Async XLA Ops:
  0.6 105.6 %copy-start = (bf16[1024,1024]{1,0:T(8,128)(2,1)S(1)}, bf16[1024,1024]{1,0:T(8,128)(2,1)}, u32[]{:S(2)}) copy-start(bf16[1024,1024]{1,0:T(8,128)(2,1)} %param.13) | copy-start | bytes 6291460
  20.4 66.4 %all-to-all-start = ((bf16[8,9,144,256]{3,2,1,0:T(8,128)(2,1)}), bf16[8,9,144,256]{3,2,1,0:T(8,128)(2,1)}, u32[]{:S(2)}, u32[]{:S(2)}) async-start(bf16[8,9,144,256]{3,2,1,0:T(8,128)(2,1)} %bitcast.51), calls=%async_computation | async-start | bytes 10616832 | tf_op jit(solution)/shard_map/all_to_all | solution.py:556
  89.6 1.6 copy-start.2
  91.2 5.8 %copy-start.13 = (bf16[1024]{0:T(1024)(128)(2,1)S(1)}, bf16[1024]{0:T(1024)(128)(2,1)}, u32[]{:S(2)}) copy-start(bf16[1024]{0:T(1024)(128)(2,1)} %param.17) | copy-start | bytes 6148
  91.2 5.9 %copy-start.12 = (bf16[9,1024]{1,0:T(8,128)(2,1)S(1)}, bf16[9,1024]{1,0:T(8,128)(2,1)}, u32[]{:S(2)}) copy-start(bf16[9,1024]{1,0:T(8,128)(2,1)} %param.16) | copy-start | bytes 55300
  91.2 69.4 %all-to-all-start.1 = ((bf16[4,10,144,256]{3,2,1,0:T(8,128)(2,1)}), bf16[4,10,144,256]{3,2,1,0:T(8,128)(2,1)}, u32[]{:S(2)}, u32[]{:S(2)}) async-start(bf16[4,10,144,256]{3,2,1,0:T(8,128)(2,1)} %bitcast.47), calls=%async_computation.1 | async-start | bytes 5898240 | tf_op jit(solution)/shard_map/all_to_all | solution.py:558
  104.6 1.6 copy-start.6
  160.6 1.6 copy-start.5
  162.2 18.0 %copy-start.10 = (bf16[1024,256]{1,0:T(8,128)(2,1)S(1)}, bf16[1024,256]{1,0:T(8,128)(2,1)}, u32[]{:S(2)}) copy-start(bf16[1024,256]{1,0:T(8,128)(2,1)} %param.14) | copy-start | bytes 1572868
  162.2 18.3 %copy-start.11 = (bf16[256,1024]{1,0:T(8,128)(2,1)S(1)}, bf16[256,1024]{1,0:T(8,128)(2,1)}, u32[]{:S(2)}) copy-start(bf16[256,1024]{1,0:T(8,128)(2,1)} %param.15) | copy-start | bytes 1572868
  180.1 3.9 copy-start.7
  183.0 8.8 %slice-start = ((s8[5898240]{0:T(1024)(128)(4,1)}), s8[4194304]{0:T(1024)(128)(4,1)S(1)}, s32[]{:S(2)}) async-start(s8[5898240]{0:T(1024)(128)(4,1)} %bitcast.52), calls=%async_computation.2 | async-start | bytes 8388608
  184.1 7.7 %slice-start.1 = ((s8[5898240]{0:T(1024)(128)(4,1)}), s8[1703936]{0:T(1024)(128)(4,1)S(1)}, s32[]{:S(2)}) async-start(s8[5898240]{0:T(1024)(128)(4,1)} %bitcast.52), calls=%async_computation.3 | async-start | bytes 3407872
  184.1 7.7 %copy-start.8 = (bf16[10,144,1024]{2,1,0:T(8,128)(2,1)S(1)}, bf16[10,144,1024]{2,1,0:T(8,128)(2,1)}, u32[]{:S(2)}) copy-start(bf16[10,144,1024]{2,1,0:T(8,128)(2,1)} %get-tuple-element.26.pooled_ref) | copy-start | bytes 8847364
  191.8 4.9 %copy-start.3 = (bf16[1024,1024]{0,1:T(8,128)(2,1)S(1)}, bf16[1024,1024]{0,1:T(8,128)(2,1)}, u32[]{:S(2)}) copy-start(bf16[1024,1024]{0,1:T(8,128)(2,1)} %copy.30) | copy-start | bytes 6291460
  301.1 5.3 %copy-start.9 = (bf16[8,128,1024]{2,1,0:T(8,128)(2,1)S(1)}, bf16[8,128,1024]{2,1,0:T(8,128)(2,1)}, u32[]{:S(2)}) copy-start(bf16[8,128,1024]{2,1,0:T(8,128)(2,1)} %get-tuple-element.38) | copy-start | bytes 6291460
  307.5 1.8 copy-start.4
  379.3 15.1 %copy-start.1 = (bf16[1024,1024]{1,0:T(8,128)(2,1)S(1)}, bf16[1024,1024]{1,0:T(8,128)(2,1)}, u32[]{:S(2)}) copy-start(bf16[1024,1024]{1,0:T(8,128)(2,1)} %param.13) | copy-start | bytes 6291460
where the time goes:
time: 397 us; the launch traced here: 394 us
  Pallas kernels  210 us (53%)
  waiting for transfers between devices  110 us (28%)
  matrix products  29.1 us (7%)
  other arithmetic  18.5 us (5%)
  local copies, waits for them, and re-layouts  15.4 us (4%)
  starting transfers between devices  10.9 us (3%)
    pallas_call x2, Pallas kernels, exchange(): pl.pallas_call(functools.partial(exchange_kernel, axes, sizes), out_shape...  130 us
    all_to_all x1, waiting for transfers between devices, local(): lax.all_to_all(send, 'enc', split_axis=0, concat_axis=0, tiled=True)  61.1 us
    all_to_all x1, waiting for transfers between devices, local(): lax.all_to_all(compact.reshape(columns, owned_rows, cells, narrow), 'abs'...  49.1 us
    pallas_call x1, Pallas kernels, backward_call(): pl.pallas_call(backward_kernel, out_shape=(jax.ShapeDtypeStruct((count, c...  26.4 us
    pallas_call x1, Pallas kernels, forward_call(): pl.pallas_call(forward_kernel, out_shape=(wide(jnp.bfloat16), wide(jnp.bf...  17.9 us
    pallas_call x1, Pallas kernels, pick_and_spread(): pl.pallas_call(spread_kernel, out_shape=jax.ShapeDtypeStruct((count, grid...  15.1 us
    pallas_call x1, Pallas kernels, pool_and_place(): pl.pallas_call(pool_kernel, out_shape=jax.ShapeDtypeStruct((sends, cells,...  15.1 us
    unnamed x33, local copies, waits for them, and re-layouts  10.7 us
  transfers between devices with their start and end apart: 2, of which 2 were waited for; matrix products, arithmetic and copies ran while one was open for 3% of the time, Pallas kernels for 0%

commit v1 on v0

--- a/solution.py
+++ b/solution.py
@@ -43,7 +43,11 @@
     return pltpu.CompilerParams(vmem_limit_bytes=VMEM_BYTES)
 
 
-def pool_kernel(rows_ref, tile_ref, out_ref, half_ref):
+def first_cells(cells):
+    return (cells // 16 + 1) // 2 * 16
+
+
+def pool_kernel(rows_ref, tile_ref, out_ref, rest_ref, half_ref):
     grid, channels = tile_ref.shape[1], tile_ref.shape[3]
     side = grid // 2
     wide = tile_ref[0].astype(jnp.float32).reshape(side, 2, grid, channels)
@@ -54,20 +58,29 @@
         half_ref[part] = half[:, lanes]
         even = half_ref[part, pl.ds(0, cells, stride=2), :]
         odd = half_ref[part, pl.ds(1, cells, stride=2), :]
-        out_ref[0, :, lanes] = ((even + odd) * 0.25).astype(jnp.bfloat16)
+        pooled = ((even + odd) * 0.25).astype(jnp.bfloat16)
+        cut = out_ref.shape[1]
+        out_ref[0, :, lanes] = pooled[:cut]
+        rest_ref[0, :, lanes] = pooled[cut:]
 
 
 def pool_and_place(tiles, rows, sends):
     count, grid, _, channels = tiles.shape
     cells = (grid // 2) ** 2
+    parts = (first_cells(cells), cells - first_cells(cells))
     return pl.pallas_call(
         pool_kernel,
-        out_shape=jax.ShapeDtypeStruct((sends, cells, channels), jnp.bfloat16),
+        out_shape=[
+            jax.ShapeDtypeStruct((sends, part, channels), jnp.bfloat16) for part in parts
+        ],
         grid_spec=pltpu.PrefetchScalarGridSpec(
             num_scalar_prefetch=1,
             grid=(count,),
             in_specs=[pl.BlockSpec((1, grid, grid, channels), lambda g, rows: (g, 0, 0, 0))],
-            out_specs=pl.BlockSpec((1, cells, channels), lambda g, rows: (rows[g], 0, 0)),
+            out_specs=[
+                pl.BlockSpec((1, part, channels), lambda g, rows: (rows[g], 0, 0))
+                for part in parts
+            ],
             scratch_shapes=[pltpu.VMEM((channels // LANES, 2 * cells, LANES), jnp.float32)],
         ),
         compiler_params=params(),
@@ -279,19 +292,21 @@
 
 
 def forward_kernel(
-    live_ref, owned_ref, back_ref, w_in_ref, kernel_ref, gain_ref,
+    live_ref, owned_ref, rest_ref, back_ref, w_in_ref, kernel_ref, gain_ref,
     pooled_ref, normed_ref, hidden_ref, spatial_ref, squeeze_ref, excite_ref,
 ):
-    columns, batch, cells, narrow = owned_ref.shape
+    columns, batch, cut, narrow = owned_ref.shape
+    cells = cut + rest_ref.shape[2]
     width = columns * narrow
     side = math.isqrt(cells)
     first = pl.program_id(0) * batch
     gain = gain_ref[...].astype(jnp.float32)
     for b in range(batch):
         keep = live_ref[first + b] > 0
-        for r in range(0, cells, ROWS):
-            rows = slice(r, r + ROWS)
-            pieces = [owned_ref[c, b, rows, :] for c in range(columns)]
+        for r in range(0, cells, 16):
+            rows = slice(r, r + 16)
+            source, at = (owned_ref, r) if r < cut else (rest_ref, r - cut)
+            pieces = [source[c, b, at : at + 16, :] for c in range(columns)]
             pooled = jnp.concatenate(pieces, axis=-1)
             wide = jnp.where(keep, pooled.astype(jnp.float32), 0.0)
             pooled_ref[b, rows, :] = wide.astype(jnp.bfloat16)
@@ -329,8 +344,9 @@
             )
 
 
-def forward_call(owned, back_scaled, live, w_in, taps, gain):
-    columns, count, cells, narrow = owned.shape
+def forward_call(owned, rest, back_scaled, live, w_in, taps, gain):
+    columns, count, cut, narrow = owned.shape
+    cells = cut + rest.shape[2]
     width = columns * narrow
     batch = 2 if count % 2 == 0 else 1
     block = lambda: pl.BlockSpec((batch, cells, width), lambda g, live: (g, 0, 0))
@@ -347,7 +363,8 @@
             num_scalar_prefetch=1,
             grid=(count // batch,),
             in_specs=[
-                pl.BlockSpec((columns, batch, cells, narrow), lambda g, live: (0, g, 0, 0)),
+                pl.BlockSpec((columns, batch, cut, narrow), lambda g, live: (0, g, 0, 0)),
+                pl.BlockSpec((columns, batch, cells - cut, narrow), lambda g, live: (0, g, 0, 0)),
                 block(), whole(w_in), whole(taps), whole(gain),
             ],
             out_specs=[block(), block(), block(), block(), row(), row()],
@@ -359,7 +376,7 @@
             transcendentals=4 * count * cells * width,
         ),
         name="forward",
-    )(live, owned, back_scaled, w_in, taps, gain)
+    )(live, owned, rest, back_scaled, w_in, taps, gain)
 
 
 def backward_kernel(
@@ -552,18 +569,23 @@
     gain_row = gain.reshape(1, width)
 
     sends = groups * MOST
-    send = pool_and_place(tiles, unpack_rows, sends).reshape(groups, MOST, cells, narrow)
-    received = lax.all_to_all(send, "enc", split_axis=0, concat_axis=0, tiled=True)
-    compact = pick_rows(received.reshape(groups * MOST, cells, narrow), gather_rows)
-    owned = lax.all_to_all(
-        compact.reshape(columns, owned_rows, cells, narrow),
-        "abs",
-        split_axis=0,
-        concat_axis=0,
-        tiled=True,
+    sizes = {"enc": groups, "abs": columns}
+    first, second = [
+        part.reshape((groups, MOST) + part.shape[1:])
+        for part in pool_and_place(tiles, unpack_rows, sends)
+    ]
+
+    def compact(part):
+        rows = part.reshape((sends,) + part.shape[2:])
+        return pick_rows(rows, gather_rows).reshape((columns, owned_rows) + part.shape[2:])
+
+    received = lax.all_to_all(first, "enc", split_axis=0, concat_axis=0, tiled=True)
+    owned, received = exchange([compact(received), second], ("abs", "enc"), sizes, 3)
+    rest_owned = lax.all_to_all(
+        compact(received), "abs", split_axis=0, concat_axis=0, tiled=True
     )
     pooled, normed, hidden, spatial, squeeze, back_excite = forward_call(
-        owned, back_scaled, live.astype(jnp.int32), w_in, taps, gain_row
+        owned, rest_owned, back_scaled, live.astype(jnp.int32), w_in, taps, gain_row
     )
 
     exact = functools.partial(jnp.dot, precision=lax.Precision.HIGHEST)
@@ -605,7 +627,6 @@
     dest = lambda term: term.astype(jnp.bfloat16).reshape(groups, columns, -1, width)
     rest = jnp.concatenate([dest(se_down_term), dest(se_up_term), dest(small)], axis=2)
 
-    sizes = {"enc": groups, "abs": columns}
     back_narrow, *partial = exchange(
         [
             back_in,

time: 397 us -> 381 us (0.960)
  waiting for transfers between devices: 110 us -> 52.4 us
  Pallas kernels: 210 us -> 243 us
  starting transfers between devices: 10.9 us -> 16.1 us
    all_to_all x2, waiting for transfers between devices: 110 us -> 52.4 us  [the longest x1 35.8 us: local(): lax.all_to_all(first, 'enc', split_axis=0, concat_axis=0, tiled=True)]
    pallas_call x2 -> x3, Pallas kernels: 130 us -> 159 us  [exchange(): pl.pallas_call(functools.partial(exchange_kernel, axes, sizes), out_shape...]
    all_to_all x2, starting transfers between devices: 10.9 us -> 16.1 us  [the longest x1 10.9 us: local(): lax.all_to_all(compact(received), 'abs', split_axis=0, concat_axis=0, til...]
    unnamed x33 -> x35, local copies, waits for them, and re-layouts: 10.7 us -> 11.2 us
where the time goes in v1:
time: 381 us; the launch traced here: 377 us
  Pallas kernels  243 us (64%)
  waiting for transfers between devices  52.4 us (14%)
  matrix products  28.8 us (8%)
  other arithmetic  20.1 us (5%)
  starting transfers between devices  16.1 us (4%)
  local copies, waits for them, and re-layouts  15.9 us (4%)
    pallas_call x3, Pallas kernels, exchange(): pl.pallas_call(functools.partial(exchange_kernel, axes, sizes), out_shape...  159 us
    all_to_all x1, waiting for transfers between devices, local(): lax.all_to_all(first, 'enc', split_axis=0, concat_axis=0, tiled=True)  35.8 us
    pallas_call x1, Pallas kernels, backward_call(): pl.pallas_call(backward_kernel, out_shape=(jax.ShapeDtypeStruct((count, c...  26.5 us
    pallas_call x1, Pallas kernels, forward_call(): pl.pallas_call(forward_kernel, out_shape=(wide(jnp.bfloat16), wide(jnp.bf...  18.6 us
    all_to_all x1, waiting for transfers between devices, local(): lax.all_to_all(compact(received), 'abs', split_axis=0, concat_axis=0, til...  16.6 us
    pallas_call x1, Pallas kernels, pick_and_spread(): pl.pallas_call(spread_kernel, out_shape=jax.ShapeDtypeStruct((count, grid...  15.1 us
    pallas_call x1, Pallas kernels, pool_and_place(): pl.pallas_call(pool_kernel, out_shape=[jax.ShapeDtypeStruct((sends, part,...  14.9 us
    unnamed x35, local copies, waits for them, and re-layouts  11.2 us
  transfers between devices with their start and end apart: 2, of which 2 were waited for; matrix products, arithmetic and copies ran while one was open for 3% of the time, Pallas kernels for 0%

profile of v1, /device:TPU:0, one launch (start us, length us, event | category | flops | bytes accessed | tf_op | source)
XLA Modules:
  0.0 377.3 jit_solution(11052281177185459666)
XLA Ops:
  0.7 0.9 eq.59
  1.6 0.8 broadcast_in_dim.104
  2.3 0.8 lt.38
  3.4 0.9 reduce_window_sum.11
  4.2 0.9 select_reduce_fusion.4
  5.3 14.9 %pool_and_place.1 = (bf16[72,80,256]{2,1,0:T(8,128)(2,1)}, bf16[72,64,256]{2,1,0:T(8,128)(2,1)S(1)}) custom-call(s32[24]{0:T(128)S(1)} %add_subtract_fusion.rows_ref, bf16[24,24,24,256]{3,2,1,0:T(8,128)(2,1)} %tile_ref.1), custom_call_target="tpu_custom_call" | custom-call | tf_op jit(solution)/shard_map/pool_and_place/pallas_call | solution.py:71
  20.3 1.4 copy-done.5
  21.7 5.2 %all-to-all-start = ((bf16[8,9,80,256]{3,2,1,0:T(8,128)(2,1)}), bf16[8,9,80,256]{3,2,1,0:T(8,128)(2,1)}, u32[]{:S(2)}, u32[]{:S(2)}) async-start(bf16[8,9,80,256]{3,2,1,0:T(8,128)(2,1)} %bitcast.59), calls=%async_computation | async-start | bytes 5898240 | tf_op jit(solution)/shard_map/all_to_all | solution.py:582
  26.9 35.8 %all-to-all-done = bf16[8,9,80,256]{3,2,1,0:T(8,128)(2,1)} async-done(((bf16[8,9,80,256]{3,2,1,0:T(8,128)(2,1)}), bf16[8,9,80,256]{3,2,1,0:T(8,128)(2,1)}, u32[]{:S(2)}, u32[]{:S(2)}) %all-to-all-start) | async-done | bytes 2949152 | tf_op jit(solution)/shard_map/all_to_all | solution.py:582
  62.7 2.3 pick_rows.2
  65.0 1.2 copy-done.3
  66.2 33.9 %exchange.3 = (bf16[4,10,80,256]{3,2,1,0:T(8,128)(2,1)}, bf16[8,9,64,256]{3,2,1,0:T(8,128)(2,1)}) custom-call(bf16[4,10,80,256]{3,2,1,0:T(8,128)(2,1)} %bitcast.51, bf16[8,9,64,256]{3,2,1,0:T(8,128)(2,1)} %bitcast.53), custom_call_target="tpu_custom_call" | custom-call | tf_op jit(solution)/shard_map/exchange/pallas_call | solution.py:251
  100.1 1.7 copy-done.6
  101.8 4.3 %pick_rows.3 = bf16[40,64,256]{2,1,0:T(8,128)(2,1)} custom-call(s32[40]{0:T(128)S(1)} %select_reduce_fusion.5.rows_ref, bf16[72,64,256]{2,1,0:T(8,128)(2,1)S(1)} %bitcast.54), custom_call_target="tpu_custom_call" | custom-call | tf_op jit(solution)/shard_map/pick_rows/pallas_call | solution.py:140
  106.1 10.9 %all-to-all-start.1 = ((bf16[4,10,64,256]{3,2,1,0:T(8,128)(2,1)}), bf16[4,10,64,256]{3,2,1,0:T(8,128)(2,1)S(1)}, u32[]{:S(2)}, u32[]{:S(2)}) async-start(bf16[4,10,64,256]{3,2,1,0:T(8,128)(2,1)} %bitcast.5), calls=%async_computation.1 | async-start | bytes 2621440 | tf_op jit(solution)/shard_map/all_to_all | solution.py:584
  117.1 4.0 %copy.30 = bf16[1024,1024]{0,1:T(8,128)(2,1)} copy(bf16[1024,1024]{1,0:T(8,128)(2,1)} %w_in_ref.1) | data formatting | bytes 4194304 | tf_op args[1]
  121.1 0.6 select_reduce_fusion.9
  121.8 0.7 fusion.27
  122.4 2.1 broadcast_select_fusion.up_ref
  124.5 1.6 copy-done.8
  126.1 5.1 %fusion.1.back_ref = f32[10,144,1024]{2,1,0:T(8,128)} fusion(bf16[10,144,1024]{2,1,0:T(8,128)(2,1)S(1)} %broadcast_select_fusion.up_ref, bf16[1024,1024]{1,0:T(8,128)(2,1)S(1)} %copy-done), kind=kOutput, calls=%fused_computation.6 | convolution fusion | flops 3019898880 | bytes 10944512 | tf_op jit(solution)/shard_map/dot_general | solution.py:565
  131.2 16.6 %all-to-all-done.1.rest_ref = bf16[4,10,64,256]{3,2,1,0:T(8,128)(2,1)S(1)} async-done(((bf16[4,10,64,256]{3,2,1,0:T(8,128)(2,1)}), bf16[4,10,64,256]{3,2,1,0:T(8,128)(2,1)S(1)}, u32[]{:S(2)}, u32[]{:S(2)}) %all-to-all-start.1) | async-done | bytes 1310752 | tf_op jit(solution)/shard_map/all_to_all | solution.py:584
  147.8 1.4 copy-done.7
  149.2 18.6 %forward.1 = (bf16[10,144,1024]{2,1,0:T(8,128)(2,1)}, bf16[10,144,1024]{2,1,0:T(8,128)(2,1)}, f32[10,144,1024]{2,1,0:T(8,128)}, f32[10,144,1024]{2,1,0:T(8,128)}...) custom-call(s32[10]{0:T(128)S(1)} %get-tuple-element.58.live_ref, bf16[4,10,80,256]{3,2,1,0:T(8,128)(2,1)S(1)} %copy-done.7, ...), custom_call_target="tpu_custom_call" | custom-call | flops 3019898880 | bytes 44236800 | tf_op jit(solution)/shard_map/forward/pallas_call | solution.py:357
  168.5 0.5 convolution_multiply_fusion.1
  169.0 1.1 convolution_convert_fusion
  170.1 0.5 convolution_multiply_fusion
  170.6 1.0 convolution_convert_fusion.1
  171.7 7.7 %bitcast_convert_fusion = bf16[1024,1024]{1,0:T(8,128)(2,1)} fusion(bf16[10,144,1024]{2,1,0:T(8,128)(2,1)S(1)} %copy-done.9, f32[10,144,1024]{2,1,0:T(8,128)} %get-tuple-element.35.spatial_ref, f32[10,1024]{1,0:T(8,128)S(1)} %fusion.5), kind=kOutput, calls=%fused_computation.2 | convolution fusion | flops 3029794816 | bytes 10985472 | tf_op jit(solution)/shard_map/dot_general | solution.py:609
  179.4 4.7 %add_convert_fusion = bf16[10,144,1024]{2,1,0:T(8,128)(2,1)} fusion(bf16[10,144,1024]{2,1,0:T(8,128)(2,1)S(1)} %copy-done.10, bf16[1024,1024]{1,0:T(8,128)(2,1)S(1)} %copy-done, f32[10,144,1024]{2,1,0:T(8,128)S(1)} %bitcast.57, f32[10,1024]{1,0:T(8,128)S(1)} %fusion.5), kind=kOutput, calls=%fused_computation | convolution fusion | flops 3033169920 | bytes 13934592 | tf_op jit(solution)/shard_map/dot_general | solution.py:606
  184.2 26.5 %backward.1 = (bf16[10,144,1024]{2,1,0:T(8,128)(2,1)}, bf16[4,10,144,256]{3,2,1,0:T(8,128)(2,1)}, f32[9,1024]{1,0:T(8,128)S(1)}, f32[1,1024]{1,0:T(1,128)S(1)}) custom-call(bf16[10,144,1024]{2,1,0:T(8,128)(2,1)} %get-tuple-element.34.pooled_ref, f32[10,144,1024]{2,1,0:T(8,128)} %get-tuple-element.37.hidden_ref, ...), custom_call_target="tpu_custom_call" | custom-call | flops 3019898880 | bytes 44236800 | tf_op jit(solution)/shard_map/backward/pallas_call | solution.py:469
  211.5 7.5 %bitcast_convert_fusion.1 = bf16[1024,1024]{1,0:T(8,128)(2,1)} fusion(bf16[10,144,1024]{2,1,0:T(8,128)(2,1)} %get-tuple-element.40, bf16[10,144,1024]{2,1,0:T(8,128)(2,1)} %get-tuple-element.41), kind=kOutput, calls=%fused_computation.3 | convolution fusion | flops 3020947456 | bytes 7995392 | tf_op jit(solution)/shard_map/dot_general | solution.py:612
  219.1 1.5 pad_maximum_fusion.refs_3_
  220.6 64.8 %exchange.4 = (bf16[4,10,144,256]{3,2,1,0:T(8,128)(2,1)}, bf16[8,128,1024]{2,1,0:T(8,128)(2,1)}, bf16[8,128,1024]{2,1,0:T(8,128)(2,1)}, bf16[8,4,17,1024]{3,2,1,0:T(8,128)(2,1)}) custom-call(bf16[4,10,144,256]{3,2,1,0:T(8,128)(2,1)} %get-tuple-element.39.refs_0_, bf16[8,128,1024]{2,1,0:T(8,128)(2,1)} %bitcast.62, bf16[8,128,1024]{2,1,0:T(8,128)(2,1)} %bitcast.61, ...), custom_call_target="tpu_custom_call" | custom-call | tf_op jit(solution)/shard_map/exchange/pallas_call | solution.py:251
  285.4 2.6 reduce_sum.175.refs_3_
  287.9 2.7 reduce_sum.173
  290.7 2.7 reduce_sum.174
  293.4 2.5 place_rows.1
  295.9 60.3 %exchange.5 = (bf16[8,9,144,256]{3,2,1,0:T(8,128)(2,1)}, bf16[4,32,1024]{2,1,0:T(8,128)(2,1)}, bf16[4,32,1024]{2,1,0:T(8,128)(2,1)}, bf16[4,17,1024]{2,1,0:T(8,128)(2,1)}) custom-call(bf16[8,9,144,256]{3,2,1,0:T(8,128)(2,1)} %bitcast.55, bf16[4,32,1024]{2,1,0:T(8,128)(2,1)} %bitcast.63, bf16[4,32,1024]{2,1,0:T(8,128)(2,1)} %bitcast.64, ...), custom_call_target="tpu_custom_call" | custom-call | tf_op jit(solution)/shard_map/exchange/pallas_call | solution.py:251
  356.2 1.0 convert_reduce_fusion.2
  357.2 0.6 fusion.23
  357.8 0.6 slice_multiply_fusion
  358.4 0.7 mul.102
  359.1 0.6 mul.98
  359.7 1.1 convert_reduce_fusion
  360.8 0.7 broadcast_multiply_fusion
  361.5 0.7 broadcast_multiply_fusion.1
  362.2 15.1 %pick_and_spread.1 = bf16[24,24,24,256]{3,2,1,0:T(8,128)(2,1)} custom-call(s32[24]{0:T(128)S(1)} %add_subtract_fusion.rows_ref, bf16[72,144,256]{2,1,0:T(8,128)(2,1)} %bitcast.58), custom_call_target="tpu_custom_call" | custom-call | tf_op jit(solution)/shard_map/pick_and_spread/pallas_call | solution.py:108
  (59 shorter events, 2.5 us)
Async XLA Ops:
  0.6 125.5 %copy-start = (bf16[1024,1024]{1,0:T(8,128)(2,1)S(1)}, bf16[1024,1024]{1,0:T(8,128)(2,1)}, u32[]{:S(2)}) copy-start(bf16[1024,1024]{1,0:T(8,128)(2,1)} %param.13) | copy-start | bytes 6291460
  20.2 1.4 copy-start.5
  21.7 41.1 %all-to-all-start = ((bf16[8,9,80,256]{3,2,1,0:T(8,128)(2,1)}), bf16[8,9,80,256]{3,2,1,0:T(8,128)(2,1)}, u32[]{:S(2)}, u32[]{:S(2)}) async-start(bf16[8,9,80,256]{3,2,1,0:T(8,128)(2,1)} %bitcast.59), calls=%async_computation | async-start | bytes 5898240 | tf_op jit(solution)/shard_map/all_to_all | solution.py:582
  65.0 1.2 copy-start.3
  100.1 1.7 copy-start.6
  101.8 15.2 %copy-start.14 = (bf16[1024]{0:T(1024)(128)(2,1)S(1)}, bf16[1024]{0:T(1024)(128)(2,1)}, u32[]{:S(2)}) copy-start(bf16[1024]{0:T(1024)(128)(2,1)} %param.17) | copy-start | bytes 6148
  101.8 15.3 %copy-start.13 = (bf16[9,1024]{1,0:T(8,128)(2,1)S(1)}, bf16[9,1024]{1,0:T(8,128)(2,1)}, u32[]{:S(2)}) copy-start(bf16[9,1024]{1,0:T(8,128)(2,1)} %param.16) | copy-start | bytes 55300
  106.1 41.7 %all-to-all-start.1 = ((bf16[4,10,64,256]{3,2,1,0:T(8,128)(2,1)}), bf16[4,10,64,256]{3,2,1,0:T(8,128)(2,1)S(1)}, u32[]{:S(2)}, u32[]{:S(2)}) async-start(bf16[4,10,64,256]{3,2,1,0:T(8,128)(2,1)} %bitcast.5), calls=%async_computation.1 | async-start | bytes 2621440 | tf_op jit(solution)/shard_map/all_to_all | solution.py:584
  124.5 1.6 copy-start.8
  147.8 1.4 copy-start.7
  149.2 18.6 %copy-start.11 = (bf16[1024,256]{1,0:T(8,128)(2,1)S(1)}, bf16[1024,256]{1,0:T(8,128)(2,1)}, u32[]{:S(2)}) copy-start(bf16[1024,256]{1,0:T(8,128)(2,1)} %param.14) | copy-start | bytes 1572868
  149.2 18.9 %copy-start.12 = (bf16[256,1024]{1,0:T(8,128)(2,1)S(1)}, bf16[256,1024]{1,0:T(8,128)(2,1)}, u32[]{:S(2)}) copy-start(bf16[256,1024]{1,0:T(8,128)(2,1)} %param.15) | copy-start | bytes 1572868
  167.8 3.9 %copy-start.9 = (bf16[10,144,1024]{2,1,0:T(8,128)(2,1)S(1)}, bf16[10,144,1024]{2,1,0:T(8,128)(2,1)}, u32[]{:S(2)}) copy-start(bf16[10,144,1024]{2,1,0:T(8,128)(2,1)} %copy-done.8) | copy-start | bytes 8847364
  170.6 8.8 %slice-start = ((s8[5898240]{0:T(1024)(128)(4,1)}), s8[4194304]{0:T(1024)(128)(4,1)S(1)}, s32[]{:S(2)}) async-start(s8[5898240]{0:T(1024)(128)(4,1)} %bitcast.56), calls=%async_computation.2 | async-start | bytes 8388608
  171.7 7.7 %slice-start.1 = ((s8[5898240]{0:T(1024)(128)(4,1)}), s8[1703936]{0:T(1024)(128)(4,1)S(1)}, s32[]{:S(2)}) async-start(s8[5898240]{0:T(1024)(128)(4,1)} %bitcast.56), calls=%async_computation.3 | async-start | bytes 3407872
  171.7 7.7 %copy-start.10 = (bf16[10,144,1024]{2,1,0:T(8,128)(2,1)S(1)}, bf16[10,144,1024]{2,1,0:T(8,128)(2,1)}, u32[]{:S(2)}) copy-start(bf16[10,144,1024]{2,1,0:T(8,128)(2,1)} %get-tuple-element.34.pooled_ref) | copy-start | bytes 8847364
  179.4 4.8 %copy-start.2 = (bf16[1024,1024]{0,1:T(8,128)(2,1)S(1)}, bf16[1024,1024]{0,1:T(8,128)(2,1)}, u32[]{:S(2)}) copy-start(bf16[1024,1024]{0,1:T(8,128)(2,1)} %copy.30) | copy-start | bytes 6291460
  285.3 8.0 %copy-start.4 = (bf16[4,10,144,256]{3,2,1,0:T(8,128)(2,1)S(1)}, bf16[4,10,144,256]{3,2,1,0:T(8,128)(2,1)}, u32[]{:S(2)}) copy-start(bf16[4,10,144,256]{3,2,1,0:T(8,128)(2,1)} %get-tuple-element.44) | copy-start | bytes 8847364
  362.2 15.1 %copy-start.1 = (bf16[1024,1024]{1,0:T(8,128)(2,1)S(1)}, bf16[1024,1024]{1,0:T(8,128)(2,1)}, u32[]{:S(2)}) copy-start(bf16[1024,1024]{1,0:T(8,128)(2,1)} %param.13) | copy-start | bytes 6291460
